TPU v7x, 32 devices: a whole 2x2x4 slice. The times are simulated.
32 devices in a mesh: groups: 2 (over x), seq: 16 (over z, y, core).
Axes of the slice: x: 2, y: 2, z: 4, core: 2. Of those that a mesh axis runs over, the one named last changes fastest.
Arguments:
- qkv: bfloat16 [4096, 4096], P('seq', 'groups'), parts along dimension 1, may hold values from -6 to 6
- igate: float32 [4, 4096], P(None, ('groups', 'seq')), parts along dimension 1, may hold values from -110 to 100
- fgate: float32 [4, 4096], P(None, ('groups', 'seq')), parts along dimension 1, may hold values from 0 to 16
- doc_start: int32 [4096], P(('groups', 'seq')), parts along dimension 0, may hold values 0 or 1
- lengths: int32 [32], P(('groups', 'seq')), parts along dimension 0, may hold values from 1 to 128, 1536 in all
Outputs:
- mixed_out: bfloat16 [4096, 2048], P(('groups', 'seq')), parts along dimension 0
There are 2 independent parts, one for each index of `groups`. A program takes and returns all parts, laid end to end along the dimension named above; each array names one. Nothing has to cross between parts.
Inputs may be any that keep to these rules, and one draw needn't show every extreme that they name: `lengths`: live positions of a shard come first, padding after them; the live counts of one sequence sum to 1536.
All inputs are finite; a program needn't handle non-finite values. No bound on the sum of `doc_start` on one device may be relied on, other than what follows from the above.
Results may differ from a plain program's by a relative error of at most 0.0056.
Values may be sent and summed in bfloat16 or wider, within the bound.
A program may use at most 128 MiB of HBM per device.

v0:
```python
import jax
import jax.numpy as jnp
from jax import lax
from jax.sharding import PartitionSpec as P

DK = 256
DV = 512
HEAD_COUNT_HALF = 4


empty_max = -1e30
highest = lax.Precision.HIGHEST


def local_terms(queries, key_rows, value_rows, igate, fgate, doc_start, live_count):
    head_count, key_dim, width = queries.shape
    token_position = lax.iota(jnp.int32, width)
    living = token_position < live_count
    log_forget = jnp.where(living[None, :], jax.nn.log_sigmoid(fgate), 0.0)
    running = jnp.cumsum(log_forget, axis=1)
    resets = jnp.cumsum(doc_start, axis=0)
    allowed = (
        (resets[:, None] == resets[None, :])
        & (token_position[:, None] >= token_position[None, :])
        & living[None, :]
    )
    tail_doc = (resets == resets[width - 1]) & living
    key_scale = key_dim ** (-0.5)
    sums, denoms, squares, maxima = ([], [], [], [])
    states, normals, summary_sq, summary_max = ([], [], [], [])
    for head_index in range(head_count):
        exponent = (
            running[head_index][:, None] - running[head_index][None, :] + igate[head_index][None, :]
        )
        exponent = jnp.where(allowed, exponent, empty_max)
        row_max = jnp.max(exponent, axis=1)
        weights = jnp.where(allowed, jnp.exp(exponent - row_max[:, None]), 0.0)
        scores = (
            jnp.einsum(
                "dt,ds->ts",
                queries[head_index],
                key_rows[head_index],
                preferred_element_type=jnp.float32,
            )
            * key_scale
        )
        weighted = weights * scores
        sums.append(
            jnp.einsum(
                "ts,js->tj",
                weighted.astype(jnp.bfloat16),
                value_rows[head_index],
                preferred_element_type=jnp.float32,
            )
        )
        denoms.append(jnp.sum(weighted, axis=1))
        squares.append(jnp.sum(weights * weights, axis=1))
        maxima.append(row_max)
        closing = running[head_index][width - 1] - running[head_index] + igate[head_index]
        closing = jnp.where(tail_doc, closing, empty_max)
        largest = jnp.max(closing)
        carried = jnp.where(tail_doc, jnp.exp(closing - largest), 0.0)
        scaled_keys = (key_rows[head_index] * (carried * key_scale)[None, :]).astype(jnp.bfloat16)
        states.append(
            jnp.einsum(
                "ds,js->dj", scaled_keys, value_rows[head_index], preferred_element_type=jnp.float32
            )
        )
        normals.append(jnp.sum(scaled_keys.astype(jnp.float32), axis=1))
        summary_sq.append(jnp.sum(carried * carried))
        summary_max.append(largest)
    open_flag = jnp.where(resets[width - 1] == 0, 1.0, 0.0).astype(jnp.float32).reshape(1)
    local_parts = (
        jnp.stack(sums, axis=1),
        jnp.stack(denoms, axis=1),
        jnp.stack(squares, axis=1),
        jnp.stack(maxima, axis=1),
        running.T,
        resets == 0,
        living,
    )
    summary = (
        jnp.stack(states),
        jnp.stack(normals),
        jnp.stack(summary_sq),
        jnp.stack(summary_max),
        running[:, width - 1],
        open_flag,
    )
    return (local_parts, summary)


def finish(local_parts, incoming, queries):
    sums, denoms, squares, maxima, running, first_open, living = local_parts
    state_in, normal_in, square_in, max_in = (incoming[0], incoming[1], incoming[2], incoming[3])
    incoming_exp = jnp.where(first_open[:, None], running + max_in[None, :], empty_max)
    largest = jnp.maximum(maxima, incoming_exp)
    own_scale = jnp.exp(maxima - largest)
    carry_scale = jnp.where(first_open[:, None], jnp.exp(incoming_exp - largest), 0.0)
    cross_term = jnp.einsum(
        "hdt,hdj->thj", queries, state_in.astype(jnp.bfloat16), preferred_element_type=jnp.float32
    )
    cross_den = jnp.einsum(
        "hdt,hd->th", queries, normal_in.astype(jnp.bfloat16), preferred_element_type=jnp.float32
    )
    numerator = own_scale[..., None] * sums + carry_scale[..., None] * cross_term
    denominator = own_scale * denoms + carry_scale * cross_den
    square = own_scale * own_scale * squares + carry_scale * carry_scale * square_in[None, :]
    divisor = jnp.where(living[:, None], jnp.maximum(jnp.abs(denominator), jnp.sqrt(square)), 1.0)
    result = jnp.where(living[:, None, None], numerator / divisor[..., None], 0.0)
    return result.reshape(result.shape[0], -1).astype(jnp.bfloat16)


def spread_prefix(summary):
    states, normals, sq_sum, top_sum, tails, open_flag = summary
    shards = lax.axis_size("seq")
    own_index = lax.axis_index("seq")
    head_count, key_dim, value_dim = states.shape
    row_count = head_count * key_dim // shards
    spread = lax.all_to_all(
        states.reshape(1, head_count * key_dim, value_dim),
        "seq",
        split_axis=1,
        concat_axis=0,
        tiled=True,
    )
    normal_all, square_all, top_all, tail_all, open_all = (
        lax.all_gather(normals[None], "seq", axis=0, tiled=True),
        lax.all_gather(sq_sum[None], "seq", axis=0, tiled=True),
        lax.all_gather(top_sum[None], "seq", axis=0, tiled=True),
        lax.all_gather(tails[None], "seq", axis=0, tiled=True),
        lax.all_gather(open_flag, "seq", axis=0, tiled=True),
    )
    tails_after = jnp.cumsum(tail_all, axis=0)
    before = tails_after - tail_all
    closed_after = jnp.cumsum(1.0 - open_all)
    closed_before = closed_after - (1.0 - open_all)
    shard_order = lax.iota(jnp.int32, shards)
    linked = (shard_order[:, None] < shard_order[None, :]) & (
        closed_before[None, :] - closed_after[:, None] < 0.5
    )
    exponent = top_all[:, None, :] + before[None, :, :] - tails_after[:, None, :]
    exponent = jnp.where(linked[..., None], exponent, empty_max)
    entry_max = jnp.max(exponent, axis=0)
    weight = jnp.where(linked[..., None], jnp.exp(exponent - entry_max[None]), 0.0)
    own_pick = (shard_order == own_index).astype(jnp.float32)
    own_weight = jnp.einsum("ijh,j->ih", weight, own_pick, precision=highest)
    normal_in = jnp.einsum("ih,ihd->hd", own_weight, normal_all, precision=highest)
    square_in = jnp.einsum("ih,ih->h", own_weight * own_weight, square_all, precision=highest)
    max_in = jnp.einsum("jh,j->h", entry_max, own_pick, precision=highest)
    row_head = (own_index * row_count + lax.iota(jnp.int32, row_count)) // key_dim
    head_pick = (lax.iota(jnp.int32, head_count)[:, None] == row_head[None, :]).astype(jnp.float32)
    row_weight = jnp.einsum("ijh,hr->jir", weight, head_pick, precision=highest)
    state_rows = jnp.einsum("jir,irc->jrc", row_weight, spread, precision=highest)
    returned = lax.all_to_all(
        state_rows.astype(jnp.bfloat16), "seq", split_axis=0, concat_axis=1, tiled=True
    ).astype(state_rows.dtype)
    return (returned.reshape(head_count, key_dim, value_dim), normal_in, square_in, max_in)


def body(qkv, igate, fgate, doc_start, lengths):
    regrouped = lax.all_to_all(qkv, "seq", split_axis=1, concat_axis=0, tiled=True)
    width = igate.shape[1]
    queries = regrouped[: HEAD_COUNT_HALF * DK].reshape(HEAD_COUNT_HALF, DK, width)
    key_rows = regrouped[HEAD_COUNT_HALF * DK : 2 * HEAD_COUNT_HALF * DK].reshape(
        HEAD_COUNT_HALF, DK, width
    )
    value_rows = regrouped[2 * HEAD_COUNT_HALF * DK :].reshape(HEAD_COUNT_HALF, DV, width)
    local_parts, summary = local_terms(
        queries, key_rows, value_rows, igate, fgate, doc_start, lengths[0]
    )
    incoming = spread_prefix(summary)
    return finish(local_parts, incoming, queries)


def solution(mesh):
    placed = (
        P("seq", "groups"),
        P(None, ("groups", "seq")),
        P(None, ("groups", "seq")),
        P(("groups", "seq")),
        P(("groups", "seq")),
    )
    return jax.shard_map(
        body, mesh=mesh, in_specs=placed, out_specs=P(("groups", "seq"), None), check_vma=False
    )
```

profile of v0, /device:TPU:29, one launch (start us, length us, event | category | flops | bytes accessed | tf_op | source)
XLA Modules:
  0.0 193.4 jit_solution(6349520891350310773)
XLA Ops:
  0.0 1.5 copy.22
  1.5 1.3 copy.23
  2.8 6.3 %all-to-all-start = ((bf16[256,16,128]{2,0,1:T(8,128)(2,1)}), bf16[256,16,128]{2,0,1:T(8,128)(2,1)S(1)}, u32[]{:S(2)}, u32[]{:S(2)}) async-start(bf16[256,16,128]{2,0,1:T(8,128)(2,1)} %copy.23), calls=%async_computation | async-start | bytes 2097152 | tf_op jit(solution)/shard_map/all_to_all | solution.py:162
  12.5 1.8 fusion.89
  14.4 3.1 %fusion.90 = (f32[]{:T(128)}, f32[128]{0:T(128)}, f32[]{:T(128)}, f32[128]{0:T(128)}, f32[]{:T(128)}, /*index=5*/f32[128]{0:T(128)}) fusion(pred[128]{0:T(512)(128)(4,1)S(1)} %get-tuple-element.31, f32[4,128]{1,0:T(4,128)S(1)} %copy-done.6, f32[4,128]{1,0:T(4,128)S(1)} %reduce_window_sum.36, f32[]{:T(128)} %bitcast.22, f32[]{:T(128)} %bitcast.26, f32[]{:T(128)} %bitcast.24), kind=kLoop, calls=%fused_computation.174 | loop fusion | flops 1533 | bytes 4760 | tf_op jit(solution)/shard_map/reduce_max | solution.py:61
  17.5 1.8 multiply_bitcast_fusion.3
  19.3 3.8 %multiply_bitcast_fusion.2 = (f32[128]{0:T(128)S(1)}, f32[128]{0:T(128)S(1)}, f32[128]{0:T(128)S(1)}) fusion(pred[1,128]{1,0:T(4,128)(4,1)S(1)} %get-tuple-element.28, f32[4,128]{1,0:T(4,128)S(1)} %copy-done.6, f32[4,128]{1,0:T(4,128)S(1)} %reduce_window_sum.36, f32[]{:T(128)} %get-tuple-element.32, f32[]{:T(128)} %bitcast.22, f32[]{:T(128)} %get-tuple-element.47, ...), kind=kLoop, calls=%fused_computation.153 | loop fusion | flops 2304 | bytes 4760 | tf_op jit(solution)/shard_map/mul | solution.py:63
  23.2 10.0 %all-to-all-done = bf16[256,16,128]{2,0,1:T(8,128)(2,1)S(1)} async-done(((bf16[256,16,128]{2,0,1:T(8,128)(2,1)}), bf16[256,16,128]{2,0,1:T(8,128)(2,1)S(1)}, u32[]{:S(2)}, u32[]{:S(2)}) %all-to-all-start) | async-done | bytes 1048608 | tf_op jit(solution)/shard_map/all_to_all | solution.py:162
  34.4 3.5 %copy.24 = f32[1,1024,512]{2,0,1:T(1,128)} copy(f32[1,1024,512]{2,1,0:T(8,128)S(1)} %bitcast.252) | data formatting | bytes 4194304 | tf_op jit(solution)/shard_map/reshape | solution.py:121
  37.9 6.0 %all-to-all-start.1 = ((f32[1,1024,512]{2,0,1:T(1,128)}), f32[1,1024,512]{2,0,1:T(1,128)S(1)}, u32[]{:S(2)}, u32[]{:S(2)}) async-start(f32[1,1024,512]{2,0,1:T(1,128)} %copy.24), calls=%async_computation.1 | async-start | bytes 4194304 | tf_op jit(solution)/shard_map/all_to_all | solution.py:120
  49.3 1.8 dynamic-update-slice
  51.0 4.0 %multiply_reduce_fusion.7 = (f32[]{:T(128)}, f32[]{:T(128)}, f32[]{:T(128)}, f32[]{:T(128)}) fusion(pred[128]{0:T(512)(128)(4,1)S(1)} %get-tuple-element.31, f32[128]{0:T(128)S(1)} %get-tuple-element.30, f32[]{:T(128)} %get-tuple-element.29, f32[128]{0:T(128)} %get-tuple-element.46, f32[]{:T(128)} %get-tuple-element.45, f32[128]{0:T(128)} %get-tuple-element.48, ...), kind=kLoop, calls=%fused_computation.150 | loop fusion | flops 2044 | bytes 2208 | tf_op jit(solution)/shard_map/reduce_sum | solution.py:70
  55.0 2.7 %maximum_dynamic-update-slice_fusion.1 = f32[64]{0:T(128)S(1)} fusion(f32[64]{0:T(128)S(1)} %broadcast.168.clone.2, u32[]{:T(128)} %bitcast.28, f32[1]{0:T(128)} %bitcast.92, f32[1]{0:T(128)} %bitcast.91, f32[1]{0:T(128)} %bitcast.90, f32[1]{0:T(128)} %bitcast.89), kind=kLoop, calls=%fused_computation.146 | loop fusion | flops 12 | bytes 276
  57.7 2.8 %maximum_dynamic-update-slice_fusion = f32[64]{0:T(128)S(1)} fusion(f32[64]{0:T(128)S(1)} %broadcast.168.clone.1, u32[]{:T(128)} %bitcast.28, f32[1]{0:T(128)} %bitcast.27, f32[1]{0:T(128)} %bitcast.25, f32[1]{0:T(128)} %bitcast.23, f32[1]{0:T(128)} %bitcast.21), kind=kLoop, calls=%fused_computation.145 | loop fusion | flops 12 | bytes 276
  60.5 41.5 %all-reduce.4 = (f32[64]{0:T(128)S(1)}, f32[64]{0:T(128)}, f32[16]{0:T(128)}, f32[64]{0:T(128)}) all-reduce(f32[64]{0:T(128)} %dynamic-update-slice.2, f32[64]{0:T(128)S(1)} %maximum_dynamic-update-slice_fusion, f32[16]{0:T(128)} %dynamic-update-slice, ...), channel_id=3, replica_groups=mesh['groups'=2,'seq'=16] {'seq'}, use_global_device_ids=true, to_apply=%add.2 | all-reduce | flops 208 | bytes 1664
  106.7 1.4 reshape.234
  108.1 1.3 reduce-window.9
  109.4 1.4 reduce.2
  115.3 1.3 copy.35
  116.6 1.4 copy.36
  118.0 1.3 reshape.237
  119.3 1.8 convolution_bitcast_fusion.9
  121.1 1.9 %copy.26 = f32[16,16,64]{1,0,2:T(8,128)} copy(f32[16,16,64]{2,0,1:T(8,128)} %convolution_bitcast_fusion.9) | data formatting | bytes 131072 | tf_op jit(solution)/shard_map/ijh,hr->jir/transpose | solution.py:153
  123.0 1.4 convolution_bitcast_fusion.10
  126.0 1.5 multiply_reduce_fusion.3
  127.5 1.5 multiply_reduce_fusion.2
  131.0 23.2 %all-gather.4 = f32[16,4,256]{2,1,0:T(4,128)} all-gather(f32[1,4,256]{2,1,0:T(4,128)S(1)} %maximum_bitcast_fusion), channel_id=4, replica_groups=mesh['groups'=2,'seq'=16] {'seq'}, dimensions={0}, use_global_device_ids=true | all-gather | bytes 69632 | tf_op jit(solution)/shard_map/all_gather | solution.py:128
  155.3 3.1 %fusion.5 = bf16[16,64,512]{2,0,1:T(8,128)(2,1)S(1)} fusion(f32[16,16,64]{1,0,2:T(8,128)S(1)} %copy-done, f32[16,64,512]{2,1,0:T(8,128)S(1)} %bitcast.251), kind=kOutput, calls=%fused_computation.4 | convolution fusion | flops 101187584 | bytes 3211264 | tf_op jit(solution)/shard_map/jir,irc->jrc/dot_general | solution.py:154
  158.5 1.6 copy.27
  160.1 6.7 %all-to-all-start.2 = ((bf16[16,64,512]{2,1,0:T(8,128)(2,1)}), bf16[16,64,512]{2,1,0:T(8,128)(2,1)S(1)}, u32[]{:S(2)}, u32[]{:S(2)}) async-start(bf16[16,64,512]{2,1,0:T(8,128)(2,1)} %copy.27), calls=%async_computation.2 | async-start | bytes 2097152 | tf_op jit(solution)/shard_map/all_to_all | solution.py:155
  169.9 20.7 %all-to-all-done.2 = bf16[16,64,512]{2,1,0:T(8,128)(2,1)S(1)} async-done(((bf16[16,64,512]{2,1,0:T(8,128)(2,1)}), bf16[16,64,512]{2,1,0:T(8,128)(2,1)S(1)}, u32[]{:S(2)}, u32[]{:S(2)}) %all-to-all-start.2) | async-done | bytes 1048608 | tf_op jit(solution)/shard_map/all_to_all | solution.py:155
  190.7 1.4 fusion.12
  (137 shorter events, 26.2 us)
Async XLA Ops:
  1.5 7.7 %copy-start.24 = (s32[128]{0:T(128)S(1)}, s32[128]{0:T(128)}, u32[]{:S(2)}) copy-start(s32[128]{0:T(128)} %param.8) | copy-start | bytes 1540
  1.5 9.3 %copy-start.21 = (f32[4,128]{1,0:T(4,128)S(1)}, f32[4,128]{1,0:T(4,128)}, u32[]{:S(2)}) copy-start(f32[4,128]{1,0:T(4,128)} %param.7) | copy-start | bytes 6148
  1.5 11.0 %copy-start.6 = (f32[4,128]{1,0:T(4,128)S(1)}, f32[4,128]{1,0:T(4,128)}, u32[]{:S(2)}) copy-start(f32[4,128]{1,0:T(4,128)} %param.6) | copy-start | bytes 6148
  2.8 30.3 %all-to-all-start = ((bf16[256,16,128]{2,0,1:T(8,128)(2,1)}), bf16[256,16,128]{2,0,1:T(8,128)(2,1)S(1)}, u32[]{:S(2)}, u32[]{:S(2)}) async-start(bf16[256,16,128]{2,0,1:T(8,128)(2,1)} %copy.23), calls=%async_computation | async-start | bytes 2097152 | tf_op jit(solution)/shard_map/all_to_all | solution.py:162
  9.6 23.5 %copy-start.7 = (s32[128]{0:T(128)}, s32[128]{0:T(128)S(1)}, u32[]{:S(2)}) copy-start(s32[128]{0:T(128)S(1)} %reduce.1) | copy-start | bytes 1540
  10.8 22.3 %copy-start.14 = (pred[128]{0:T(512)(128)(4,1)}, pred[128]{0:T(512)(128)(4,1)S(1)}, u32[]{:S(2)}) copy-start(pred[128]{0:T(512)(128)(4,1)S(1)} %iota_compare_fusion.3) | copy-start | bytes 388
  19.3 15.0 %copy-start.10 = (f32[128]{0:T(128)}, f32[128]{0:T(128)S(1)}, u32[]{:S(2)}) copy-start(f32[128]{0:T(128)S(1)} %get-tuple-element.27) | copy-start | bytes 1540
  23.1 11.2 %copy-start.11 = (f32[128]{0:T(128)}, f32[128]{0:T(128)S(1)}, u32[]{:S(2)}) copy-start(f32[128]{0:T(128)S(1)} %get-tuple-element.42) | copy-start | bytes 1540
  23.2 11.2 %copy-start.12 = (f32[128]{0:T(128)}, f32[128]{0:T(128)S(1)}, u32[]{:S(2)}) copy-start(f32[128]{0:T(128)S(1)} %get-tuple-element.43) | copy-start | bytes 1540
  23.2 11.2 %copy-start.13 = (f32[128]{0:T(128)}, f32[128]{0:T(128)S(1)}, u32[]{:S(2)}) copy-start(f32[128]{0:T(128)S(1)} %get-tuple-element.44) | copy-start | bytes 1540
  37.9 13.2 %copy-start.23 = (f32[128]{0:T(128)S(1)}, f32[128]{0:T(128)}, u32[]{:S(2)}) copy-start(f32[128]{0:T(128)} %get-tuple-element.33) | copy-start | bytes 1540
  37.9 116.4 %all-to-all-start.1 = ((f32[1,1024,512]{2,0,1:T(1,128)}), f32[1,1024,512]{2,0,1:T(1,128)S(1)}, u32[]{:S(2)}, u32[]{:S(2)}) async-start(f32[1,1024,512]{2,0,1:T(1,128)} %copy.24), calls=%async_computation.1 | async-start | bytes 4194304 | tf_op jit(solution)/shard_map/all_to_all | solution.py:120
  126.0 5.0 %copy-start.18 = (f32[128]{0:T(128)}, f32[128]{0:T(128)S(1)}, u32[]{:S(2)}) copy-start(f32[128]{0:T(128)S(1)} %fusion.41) | copy-start | bytes 1540
  158.4 8.4 %copy-start.3 = (f32[16,4,256]{2,1,0:T(4,128)S(1)}, f32[16,4,256]{2,1,0:T(4,128)}, u32[]{:S(2)}) copy-start(f32[16,4,256]{2,1,0:T(4,128)} %all-gather.4) | copy-start | bytes 196612
  158.4 8.4 %copy-start.9 = (f32[16,4,1]{0,2,1:T(1,128)S(1)}, f32[16,4,1]{0,2,1:T(1,128)}, u32[]{:S(2)}) copy-start(f32[16,4,1]{0,2,1:T(1,128)} %copy.36) | copy-start | bytes 772
  158.4 8.6 %copy-start.8 = (s32[128]{0:T(128)S(1)}, s32[128]{0:T(128)}, u32[]{:S(2)}) copy-start(s32[128]{0:T(128)} %copy-done.7) | copy-start | bytes 1540
  158.4 8.6 %copy-start.15 = (pred[128]{0:T(512)(128)(4,1)S(1)}, pred[128]{0:T(512)(128)(4,1)}, u32[]{:S(2)}) copy-start(pred[128]{0:T(512)(128)(4,1)} %copy-done.14) | copy-start | bytes 388
  158.4 8.6 %copy-start.29 = (f32[128]{0:T(128)S(1)}, f32[128]{0:T(128)}, u32[]{:S(2)}) copy-start(f32[128]{0:T(128)} %get-tuple-element.49) | copy-start | bytes 1540
  158.5 8.6 %copy-start.30 = (f32[128]{0:T(128)S(1)}, f32[128]{0:T(128)}, u32[]{:S(2)}) copy-start(f32[128]{0:T(128)} %get-tuple-element.50) | copy-start | bytes 1540
  158.5 8.6 %copy-start.37 = (f32[128]{0:T(128)S(1)}, f32[128]{0:T(128)}, u32[]{:S(2)}) copy-start(f32[128]{0:T(128)} %copy-done.36) | copy-start | bytes 1540
  158.5 8.8 %copy-start.2 = (bf16[2,256,128]{2,1,0:T(8,128)(2,1)S(1)}, bf16[2,256,128]{2,1,0:T(8,128)(2,1)}, u32[]{:S(2)}) copy-start(bf16[2,256,128]{2,1,0:T(8,128)(2,1)} %copy-done.1) | copy-start | bytes 393220
  158.5 9.1 %copy-start.27 = (f32[128]{0:T(128)S(1)}, f32[128]{0:T(128)}, u32[]{:S(2)}) copy-start(f32[128]{0:T(128)} %get-tuple-element.51) | copy-start | bytes 1540
  158.5 9.1 %copy-start.28 = (f32[128]{0:T(128)S(1)}, f32[128]{0:T(128)}, u32[]{:S(2)}) copy-start(f32[128]{0:T(128)} %get-tuple-element.54) | copy-start | bytes 1540
  158.5 9.1 %copy-start.35 = (f32[128]{0:T(128)S(1)}, f32[128]{0:T(128)}, u32[]{:S(2)}) copy-start(f32[128]{0:T(128)} %copy-done.34) | copy-start | bytes 1540
  160.1 7.9 %copy-start.25 = (f32[128]{0:T(128)S(1)}, f32[128]{0:T(128)}, u32[]{:S(2)}) copy-start(f32[128]{0:T(128)} %get-tuple-element.52) | copy-start | bytes 1540
  160.1 7.9 %copy-start.26 = (f32[128]{0:T(128)S(1)}, f32[128]{0:T(128)}, u32[]{:S(2)}) copy-start(f32[128]{0:T(128)} %get-tuple-element.55) | copy-start | bytes 1540
  160.1 8.0 %copy-start.33 = (f32[128]{0:T(128)S(1)}, f32[128]{0:T(128)}, u32[]{:S(2)}) copy-start(f32[128]{0:T(128)} %copy-done.32) | copy-start | bytes 1540
  160.1 9.1 %copy-start.16 = (f32[128]{0:T(128)S(1)}, f32[128]{0:T(128)}, u32[]{:S(2)}) copy-start(f32[128]{0:T(128)} %get-tuple-element.56) | copy-start | bytes 1540
  160.1 9.1 %copy-start.17 = (f32[128]{0:T(128)S(1)}, f32[128]{0:T(128)}, u32[]{:S(2)}) copy-start(f32[128]{0:T(128)} %get-tuple-element.53) | copy-start | bytes 1540
  160.1 9.1 %copy-start.19 = (f32[128]{0:T(128)S(1)}, f32[128]{0:T(128)}, u32[]{:S(2)}) copy-start(f32[128]{0:T(128)} %copy-done.18) | copy-start | bytes 1540
  160.1 30.5 %all-to-all-start.2 = ((bf16[16,64,512]{2,1,0:T(8,128)(2,1)}), bf16[16,64,512]{2,1,0:T(8,128)(2,1)S(1)}, u32[]{:S(2)}, u32[]{:S(2)}) async-start(bf16[16,64,512]{2,1,0:T(8,128)(2,1)} %copy.27), calls=%async_computation.2 | async-start | bytes 2097152 | tf_op jit(solution)/shard_map/all_to_all | solution.py:155
  166.8 3.0 %copy-start.20 = (pred[128]{0:T(512)(128)(4,1)S(1)}, pred[128]{0:T(512)(128)(4,1)}, u32[]{:S(2)}) copy-start(pred[128]{0:T(512)(128)(4,1)} %broadcast_compare_fusion) | copy-start | bytes 388
  (12 other events, 24.1 us)
where the time goes:
time: 196 us; the launch traced here: 193 us
  blocking collectives  64.7 us (33%)
  other arithmetic  36.7 us (19%)
  waiting for transfers between devices  30.7 us (16%)
  local copies, waits for them, and re-layouts  27.7 us (14%)
  starting transfers between devices  19 us (10%)
  matrix products  12.1 us (6%)
  between operations  2.49 us (1%)
    unnamed x1, blocking collectives  41.5 us
    all_gather x1, blocking collectives, spread_prefix(): lax.all_gather(normals[None], 'seq', axis=0, tiled=True)  23.2 us
    all_to_all x1, waiting for transfers between devices, spread_prefix(): lax.all_to_all(state_rows.astype(jnp.bfloat16), 'seq', split_axis=0, conc...  20.7 us
    all_to_all x1, waiting for transfers between devices, body(): lax.all_to_all(qkv, 'seq', split_axis=1, concat_axis=0, tiled=True)  9.95 us
    unnamed x91, local copies, waits for them, and re-layouts  8.51 us
    all_to_all x1, starting transfers between devices, spread_prefix(): lax.all_to_all(state_rows.astype(jnp.bfloat16), 'seq', split_axis=0, conc...  6.66 us
    all_to_all x1, starting transfers between devices, body(): lax.all_to_all(qkv, 'seq', split_axis=1, concat_axis=0, tiled=True)  6.33 us
    all_to_all x1, starting transfers between devices, spread_prefix(): lax.all_to_all(states.reshape(1, head_count * key_dim, value_dim), 'seq',...  6 us
  transfers between devices with their start and end apart: 3, of which 2 were waited for; matrix products, arithmetic and copies ran while one was open for 31% of the time, Pallas kernels for 0%

commit v1 on v0

--- a/solution.py
+++ b/solution.py
@@ -1,6 +1,9 @@
+import functools
 import jax
 import jax.numpy as jnp
 from jax import lax
+from jax.experimental import pallas as pl
+from jax.experimental.pallas import tpu as pltpu
 from jax.sharding import PartitionSpec as P
 
 DK = 256
@@ -10,6 +13,12 @@
 
 empty_max = -1e30
 highest = lax.Precision.HIGHEST
+
+
+def running_sum(x):
+    spots = lax.iota(jnp.int32, x.shape[-1])
+    upto = spots[None, :] <= spots[:, None]
+    return jnp.sum(jnp.where(upto, x[..., None, :], jnp.zeros((), x.dtype)), axis=-1)
 
 
 def local_terms(queries, key_rows, value_rows, igate, fgate, doc_start, live_count):
@@ -17,8 +26,8 @@
     token_position = lax.iota(jnp.int32, width)
     living = token_position < live_count
     log_forget = jnp.where(living[None, :], jax.nn.log_sigmoid(fgate), 0.0)
-    running = jnp.cumsum(log_forget, axis=1)
-    resets = jnp.cumsum(doc_start, axis=0)
+    running = running_sum(log_forget)
+    resets = running_sum(doc_start)
     allowed = (
         (resets[:, None] == resets[None, :])
         & (token_position[:, None] >= token_position[None, :])
@@ -131,9 +140,9 @@
         lax.all_gather(tails[None], "seq", axis=0, tiled=True),
         lax.all_gather(open_flag, "seq", axis=0, tiled=True),
     )
-    tails_after = jnp.cumsum(tail_all, axis=0)
+    tails_after = running_sum(tail_all.T).T
     before = tails_after - tail_all
-    closed_after = jnp.cumsum(1.0 - open_all)
+    closed_after = running_sum(1.0 - open_all)
     closed_before = closed_after - (1.0 - open_all)
     shard_order = lax.iota(jnp.int32, shards)
     linked = (shard_order[:, None] < shard_order[None, :]) & (
@@ -173,6 +182,275 @@
     return finish(local_parts, incoming, queries)
 
 
+MESH = pl.DeviceIdType.MESH
+f32, bf16 = jnp.float32, jnp.bfloat16
+HEADS = HEAD_COUNT_HALF
+PARTS = DV // 128
+
+
+def dot_nt(a, b):
+    return lax.dot_general(a, b, (((1,), (1,)), ((), ())), preferred_element_type=f32)
+
+
+def worker_kernel(
+    qkv, ig, fg, doc, live_len, out,
+    inbox, meta, metain, wts, qt, num, den, st_in, st_out, sm_in, sm_out, obuf,
+    insend, inrecv, msend, mrecv, csend, crecv, osend, orecv,
+):
+    planes = HEADS
+    width = ig.shape[1]
+    span = planes * width
+    g = lax.axis_index("groups")
+    d = lax.axis_index("seq")
+    p = lax.div(d, HEADS)
+    h = lax.rem(d, HEADS)
+    big = lax.div(d, 2 * HEADS)
+    hd = (1 - big) * h + big * (lax.div(d, 2) - HEADS)
+    role = (1 - big) * p + big * (2 + lax.rem(d, 2))
+    peers = [lax.rem(h + i, HEADS) for i in range(1, HEADS)]
+
+    pos = lax.broadcasted_iota(jnp.int32, (1, width), 1)
+    live = pos < live_len[0]
+    x = fg[...]
+    a = jnp.where(live, jnp.minimum(x, 0.0) - jnp.log1p(jnp.exp(-jnp.abs(x))), 0.0)
+    livef = jnp.where(live, 1.0, 0.0).astype(f32)
+    docf = doc[...].astype(f32)
+    pad = jnp.zeros((4, width), f32)
+    for i in range(HEADS):
+        meta[i] = jnp.concatenate([ig[i : i + 1, :], a[i : i + 1, :], docf, livef, pad], axis=0)
+
+    bar = pltpu.get_barrier_semaphore()
+
+    def greet(dev):
+        pl.semaphore_signal(bar, inc=1, device_id=(g, dev), device_id_type=MESH)
+
+    for s in (h, HEADS + h, 2 * HEADS + 2 * h, 2 * HEADS + 2 * h + 1):
+        pl.when(s != d)(functools.partial(greet, s))
+    for b in peers:
+        greet(HEADS * p + b)
+    pl.when(p > 0)(functools.partial(greet, d - HEADS))
+    count = 2 * HEADS - 1 + jnp.where(p < planes - 1, 1, 0) - jnp.where(hd == h, 1, 0)
+    pl.semaphore_wait(bar, count)
+
+    def remote(src, dst, ss, rs, dev):
+        return pltpu.make_async_remote_copy(
+            src_ref=src, dst_ref=dst, send_sem=ss, recv_sem=rs, device_id=(g, dev), device_id_type=MESH
+        )
+
+    mcopies = [
+        remote(meta.at[b], metain.at[h], msend.at[i], mrecv.at[h], HEADS * p + b)
+        for i, b in enumerate(peers)
+    ]
+    for c in mcopies:
+        c.start()
+    metain[h] = meta[h]
+
+    def feature(j):
+        return remote(
+            qkv.at[:, pl.ds(j * span, span)], inbox.at[role], insend.at[j], inrecv.at[role], HEADS * j + hd
+        )
+
+    for j in range(planes):
+        away = HEADS * j + hd != d
+
+        @pl.when(away)
+        def _():
+            feature(j).start()
+
+        @pl.when(jnp.logical_not(away))
+        def _():
+            pltpu.make_async_copy(
+                qkv.at[:, pl.ds(j * span, span)], inbox.at[role], inrecv.at[role]
+            ).start()
+
+    def landed(slot):
+        pltpu.make_async_copy(inbox.at[slot], inbox.at[slot], inrecv.at[slot]).wait()
+
+    for i, b in enumerate(peers):
+        pltpu.make_async_copy(metain.at[b], metain.at[b], mrecv.at[b]).wait()
+
+    rows = jnp.concatenate([metain[b] for b in range(planes)], axis=1)
+    ig_row, a_row, doc_row, live_row = (rows[i : i + 1, :] for i in range(4))
+    ti = lax.broadcasted_iota(jnp.int32, (span, span), 0)
+    si = lax.broadcasted_iota(jnp.int32, (span, span), 1)
+    tri = ti >= si
+    eye = ti == si
+    b_col = jnp.sum(jnp.where(tri, a_row, 0.0), axis=1, keepdims=True)
+    r_col = jnp.sum(jnp.where(tri, doc_row, 0.0), axis=1, keepdims=True)
+    live_col = jnp.sum(jnp.where(eye, live_row, 0.0), axis=1, keepdims=True)
+    b_row = jnp.sum(jnp.where(eye, b_col, 0.0), axis=0, keepdims=True)
+    r_row = jnp.sum(jnp.where(eye, r_col, 0.0), axis=0, keepdims=True)
+    allowed = tri & (r_col == r_row) & (live_row > 0.5)
+    ex = jnp.where(allowed, b_col - b_row + ig_row, empty_max)
+    top = jnp.max(ex, axis=1, keepdims=True)
+    weights = jnp.where(allowed, jnp.exp(ex - top), 0.0)
+    wts[...] = weights
+    sq_own = jnp.sum(weights * weights, axis=1, keepdims=True)
+    b_end = b_row[:, span - 1 : span]
+    r_end = r_row[:, span - 1 : span]
+    tail = (r_row == r_end) & (live_row > 0.5)
+    cl = jnp.where(tail, b_end - b_row + ig_row, empty_max)
+    mu = jnp.max(cl, axis=1, keepdims=True)
+    u = jnp.where(tail, jnp.exp(cl - mu), 0.0)
+    sq_sum = jnp.sum(u * u, axis=1, keepdims=True)
+    key_scale = DK ** (-0.5)
+
+    def own():
+        landed(0)
+        qt[...] = inbox[0].astype(f32).T.astype(bf16)
+        for b in range(planes):
+            r = pl.ds(b * width, width)
+            score = jnp.dot(qt[r, :], inbox[1], preferred_element_type=f32) * key_scale
+            w = wts[r, :] * score
+            den[r, :] = jnp.sum(w, axis=1, keepdims=True)
+            wb = w.astype(bf16)
+            for f in range(2):
+                num[r, pl.ds(f * DK, DK)] = dot_nt(wb, inbox[2 + f])
+
+    @pl.when(p == 0)
+    def _():
+        st_in[...] = jnp.zeros(st_in.shape, bf16)
+        sm_in[...] = jnp.concatenate(
+            [jnp.zeros((16, DK), f32), jnp.full((8, DK), empty_max, f32)], axis=0
+        )
+
+    landed(1)
+    keyw = (inbox[1].astype(f32) * (u * key_scale)).astype(bf16)
+    n8 = dot_nt(jnp.ones((8, span), bf16), keyw)
+    landed(2)
+    landed(3)
+    pl.when(p >= 2)(own)
+
+    sm_copy = remote(sm_out, sm_in, csend.at[PARTS], crecv.at[PARTS], d + HEADS)
+    st_copies = [
+        remote(st_out.at[c], st_in.at[c], csend.at[c], crecv.at[c], d + HEADS) for c in range(PARTS)
+    ]
+
+    @pl.when(p > 0)
+    def _():
+        pltpu.make_async_copy(sm_in, sm_in, crecv.at[PARTS]).wait()
+
+    m_in = sm_in[16:17, 0:1]
+    carried = b_end + m_in
+    opened = r_end < 0.5
+    largest = jnp.maximum(mu, jnp.where(opened, carried, empty_max))
+    late = jnp.exp(mu - largest)
+    early = jnp.where(opened, jnp.exp(carried - largest), 0.0)
+
+    @pl.when(p < planes - 1)
+    def _():
+        sm_out[0:8, :] = late * n8 + early * sm_in[0:8, :]
+        sm_out[8:16, :] = late * late * sq_sum + early * early * sm_in[8:16, :]
+        sm_out[16:24, :] = jnp.broadcast_to(largest, (8, DK))
+        sm_copy.start()
+
+    for c in range(PARTS):
+
+        @pl.when(p > 0)
+        def _():
+            pltpu.make_async_copy(st_in.at[c], st_in.at[c], crecv.at[c]).wait()
+
+        @pl.when(p < planes - 1)
+        def _():
+            vals = inbox[2 + c // 2, pl.ds((c % 2) * 128, 128), :]
+            st_out[c] = (late * dot_nt(keyw, vals) + early * st_in[c].astype(f32)).astype(bf16)
+            st_copies[c].start()
+
+    pl.when(p < 2)(own)
+
+    nb = sm_in[0:8, :].astype(bf16)
+    sq_in = sm_in[8:9, 0:1]
+
+    def result(b):
+        return remote(
+            obuf.at[b], out.at[:, pl.ds(pl.multiple_of(h * DV, DV), DV)], osend.at[b], orecv.at[h], HEADS * p + b
+        )
+
+    def own_result(b):
+        return pltpu.make_async_copy(
+            obuf.at[b], out.at[:, pl.ds(pl.multiple_of(h * DV, DV), DV)], orecv.at[h]
+        )
+
+    for b in range(planes):
+        lo, r = b * width, pl.ds(b * width, width)
+        first = r_col[lo : lo + width] < 0.5
+        f = jnp.where(first, b_col[lo : lo + width] + m_in, empty_max)
+        mx = top[lo : lo + width]
+        m = jnp.maximum(mx, f)
+        xs = jnp.exp(mx - m)
+        ys = jnp.where(first, jnp.exp(f - m), 0.0)
+        qb = qt[r, :]
+        dn = xs * den[r, :] + ys * dot_nt(qb, nb)[:, 0:1]
+        sq = xs * xs * sq_own[lo : lo + width] + ys * ys * sq_in
+        lv = live_col[lo : lo + width] > 0.5
+        inv = 1.0 / jnp.where(lv, jnp.maximum(jnp.abs(dn), jnp.sqrt(sq)), 1.0)
+        for c in range(PARTS):
+            cs = pl.ds(c * 128, 128)
+            cross = jnp.dot(qb, st_in[c], preferred_element_type=f32)
+            obuf[b, :, cs] = jnp.where(lv, (xs * num[r, cs] + ys * cross) * inv, 0.0).astype(bf16)
+
+        @pl.when(h != b)
+        def _():
+            result(b).start()
+
+        @pl.when(h == b)
+        def _():
+            own_result(b).start()
+
+    for i in range(HEADS):
+        here = out.at[:, pl.ds(i * DV, DV)]
+        pltpu.make_async_copy(here, here, orecv.at[i]).wait()
+    for c in mcopies:
+        c.wait_send()
+    for j in range(planes):
+
+        @pl.when(HEADS * j + hd != d)
+        def _():
+            feature(j).wait_send()
+
+        @pl.when(h != j)
+        def _():
+            result(j).wait_send()
+
+    @pl.when(p < planes - 1)
+    def _():
+        sm_copy.wait_send()
+        for c in st_copies:
+            c.wait_send()
+
+
+def worker_body(qkv, igate, fgate, doc_start, lengths):
+    width = igate.shape[1]
+    span = HEADS * width
+    vm = pl.BlockSpec(memory_space=pltpu.VMEM)
+    dma = pltpu.SemaphoreType.DMA
+    return pl.pallas_call(
+        worker_kernel,
+        out_shape=jax.ShapeDtypeStruct((width, HEADS * DV), bf16),
+        in_specs=[pl.BlockSpec(memory_space=pl.ANY), vm, vm, vm, pl.BlockSpec(memory_space=pltpu.SMEM)],
+        out_specs=pl.BlockSpec(memory_space=pl.ANY),
+        scratch_shapes=[
+            pltpu.VMEM((4, DK, span), bf16),
+            pltpu.VMEM((HEADS, 8, width), f32),
+            pltpu.VMEM((HEADS, 8, width), f32),
+            pltpu.VMEM((span, span), f32),
+            pltpu.VMEM((span, DK), bf16),
+            pltpu.VMEM((span, DV), f32),
+            pltpu.VMEM((span, 1), f32),
+            pltpu.VMEM((PARTS, DK, 128), bf16),
+            pltpu.VMEM((PARTS, DK, 128), bf16),
+            pltpu.VMEM((24, DK), f32),
+            pltpu.VMEM((24, DK), f32),
+            pltpu.VMEM((HEADS, width, DV), bf16),
+            dma((HEADS,)), dma((4,)), dma((HEADS - 1,)), dma((HEADS,)),
+            dma((PARTS + 1,)), dma((PARTS + 1,)), dma((HEADS,)), dma((HEADS,)),
+        ],
+        compiler_params=pltpu.CompilerParams(
+            collective_id=0, has_side_effects=True, vmem_limit_bytes=40 * 1024 * 1024
+        ),
+    )(qkv, igate, fgate, doc_start.reshape(1, width), lengths)
+
+
 def solution(mesh):
     placed = (
         P("seq", "groups"),
@@ -181,6 +459,8 @@
         P(("groups", "seq")),
         P(("groups", "seq")),
     )
+    shards = mesh.shape["seq"]
+    whole_heads = shards == HEADS * HEADS and shards * DK == 2 * HEADS * DK + HEADS * DV
     return jax.shard_map(
-        body, mesh=mesh, in_specs=placed, out_specs=P(("groups", "seq"), None), check_vma=False
-    )
+        worker_body if whole_heads else body, mesh=mesh, in_specs=placed, out_specs=P(("groups", "seq"), None), check_vma=False
+    )

time: 196 us -> 49.8 us (0.25); the launches traced: 193 us -> 49.6 us
  blocking collectives: 64.7 us -> 0 us
  Pallas kernels: 0 us -> 45.5 us
  other arithmetic: 36.7 us -> 0 us
  waiting for transfers between devices: 30.7 us -> 0 us
  local copies, waits for them, and re-layouts: 27.7 us -> 3.35 us
  starting transfers between devices: 19 us -> 0 us
  matrix products: 12.1 us -> 0 us
    pallas_call x0 -> x1, Pallas kernels: none -> 45.5 us  [worker_body(): pl.pallas_call(worker_kernel, out_shape=jax.ShapeDtypeStruct((width, HEAD...]
    unnamed x1 -> x0, blocking collectives: 41.5 us -> none
    all_to_all x3 -> x0, waiting for transfers between devices: 30.7 us -> none  [the longest x1 20.7 us: spread_prefix(): lax.all_to_all(state_rows.astype(jnp.bfloat16), 'seq', split_axis=0, conc...]
    all_gather x1 -> x0, blocking collectives: 23.2 us -> none  [spread_prefix(): lax.all_gather(normals[None], 'seq', axis=0, tiled=True)]
    all_to_all x3 -> x0, starting transfers between devices: 19 us -> none  [the longest x1 6.66 us: spread_prefix(): lax.all_to_all(state_rows.astype(jnp.bfloat16), 'seq', split_axis=0, conc...]
    dot_general x19 -> x0, matrix products: 12.1 us -> none  [the longest x1 3.07 us: spread_prefix(): jnp.einsum('jir,irc->jrc', row_weight, spread, precision=highest)]
    reduce_sum x4 -> x0, other arithmetic: 7.86 us -> none  [the longest x1 3.97 us: local_terms(): summary_sq.append(jnp.sum(carried * carried))]
    reduce_max x4 -> x0, other arithmetic: 6.63 us -> none  [the longest x2 4.95 us: local_terms(): largest = jnp.max(closing)]
  transfers between devices with their start and end apart: 3 -> 0, of which waited for: 2 -> 0; matrix products, arithmetic and copies ran while one was open for 31% -> 0% of each run, Pallas kernels for 0% -> 0%
where the time goes in v1:
time: 49.8 us; the launch traced here: 49.6 us
  Pallas kernels  45.5 us (91%)
  local copies, waits for them, and re-layouts  3.35 us (7%)
  between operations  0.69 us (1%)
    pallas_call x1, Pallas kernels, worker_body(): pl.pallas_call(worker_kernel, out_shape=jax.ShapeDtypeStruct((width, HEAD...  45.5 us
    unnamed x9, local copies, waits for them, and re-layouts  3.35 us

profile of v1, /device:TPU:29, one launch (start us, length us, event | category | flops | bytes accessed | tf_op | source)
XLA Modules:
  0.0 49.6 jit_solution(13217798563388782281)
XLA Ops:
  0.0 0.0 copy-start.1
  0.7 0.0 copy-start.3
  0.7 0.0 copy-done.1
  0.7 0.6 %copy-done.3 = s32[128]{0:T(128)S(1)} copy-done((s32[128]{0:T(128)S(1)}, s32[128]{0:T(128)}, u32[]{:S(2)}) %copy-start.3) | copy-done | bytes 536
  1.3 0.0 copy-start
  1.3 1.2 %copy-done = bf16[256,2048]{1,0:T(8,128)(2,1)S(1)} copy-done((bf16[256,2048]{1,0:T(8,128)(2,1)S(1)}, bf16[256,2048]{1,0:T(8,128)(2,1)}, u32[]{:S(2)}) %copy-start) | copy-done | bytes 1048600
  2.5 0.0 copy-start.2
  2.6 0.7 %copy-done.2 = f32[4,128]{1,0:T(4,128)S(1)} copy-done((f32[4,128]{1,0:T(4,128)S(1)}, f32[4,128]{1,0:T(4,128)}, u32[]{:S(2)}) %copy-start.2) | copy-done | bytes 2072
  3.2 45.5 %shard_map.55 = bf16[128,2048]{1,0:T(8,128)(2,1)S(1)} custom-call(bf16[256,2048]{1,0:T(8,128)(2,1)S(1)} %copy-done, f32[4,128]{1,0:T(4,128)S(1)} %copy-done.1, f32[4,128]{1,0:T(4,128)S(1)} %copy-done.2, s32[1,128]{1,0:T(1,128)S(1)} %bitcast.1, s32[1]{0:T(128)S(6)} %copy.7.live_len), custom_call_target="tpu_custom_call" | custom-call | tf_op jit(solution)/shard_map/pallas_call | solution.py:427
  48.8 0.8 %copy.8 = bf16[128,2048]{1,0:T(8,128)(2,1)} copy(bf16[128,2048]{1,0:T(8,128)(2,1)S(1)} %shard_map.55) | data formatting | bytes 1048576
Async XLA Ops:
  0.0 0.7 %copy-start.1 = (f32[4,128]{1,0:T(4,128)S(1)}, f32[4,128]{1,0:T(4,128)}, u32[]{:S(2)}) copy-start(f32[4,128]{1,0:T(4,128)} %ig.1) | copy-start | bytes 6148
  0.7 0.7 %copy-start.3 = (s32[128]{0:T(128)S(1)}, s32[128]{0:T(128)}, u32[]{:S(2)}) copy-start(s32[128]{0:T(128)} %param.8) | copy-start | bytes 1540
  1.3 1.2 %copy-start = (bf16[256,2048]{1,0:T(8,128)(2,1)S(1)}, bf16[256,2048]{1,0:T(8,128)(2,1)}, u32[]{:S(2)}) copy-start(bf16[256,2048]{1,0:T(8,128)(2,1)} %qkv.1) | copy-start | bytes 3145732
  2.5 0.7 %copy-start.2 = (f32[4,128]{1,0:T(4,128)S(1)}, f32[4,128]{1,0:T(4,128)}, u32[]{:S(2)}) copy-start(f32[4,128]{1,0:T(4,128)} %fg.1) | copy-start | bytes 6148

commit v2 on v1

--- a/solution.py
+++ b/solution.py
@@ -193,12 +193,12 @@
 
 
 def worker_kernel(
-    qkv, ig, fg, doc, live_len, out,
-    inbox, meta, metain, wts, qt, num, den, st_in, st_out, sm_in, sm_out, obuf,
-    insend, inrecv, msend, mrecv, csend, crecv, osend, orecv,
+    qkv, ig_hbm, fg_hbm, doc_hbm, live_len, out,
+    ig, fg, doc, inbox, meta, metain, wts, qt, num, den, st_in, st_out, sm_in, sm_out, obuf,
+    insend, inrecv, msend, mrecv, csend, crecv, osend, orecv, lsem,
 ):
     planes = HEADS
-    width = ig.shape[1]
+    width = ig_hbm.shape[1]
     span = planes * width
     g = lax.axis_index("groups")
     d = lax.axis_index("seq")
@@ -209,6 +209,26 @@
     role = (1 - big) * p + big * (2 + lax.rem(d, 2))
     peers = [lax.rem(h + i, HEADS) for i in range(1, HEADS)]
 
+    loads = [
+        pltpu.make_async_copy(src, dst, lsem.at[i])
+        for i, (src, dst) in enumerate(((ig_hbm, ig), (fg_hbm, fg), (doc_hbm, doc)))
+    ]
+    for c in loads:
+        c.start()
+
+    bar = pltpu.get_barrier_semaphore()
+
+    def greet(dev):
+        pl.semaphore_signal(bar, inc=1, device_id=(g, dev), device_id_type=MESH)
+
+    for s in (h, HEADS + h, 2 * HEADS + 2 * h, 2 * HEADS + 2 * h + 1):
+        pl.when(s != d)(functools.partial(greet, s))
+    for b in peers:
+        greet(HEADS * p + b)
+    pl.when(p > 0)(functools.partial(greet, d - HEADS))
+
+    for c in loads:
+        c.wait()
     pos = lax.broadcasted_iota(jnp.int32, (1, width), 1)
     live = pos < live_len[0]
     x = fg[...]
@@ -219,16 +239,6 @@
     for i in range(HEADS):
         meta[i] = jnp.concatenate([ig[i : i + 1, :], a[i : i + 1, :], docf, livef, pad], axis=0)
 
-    bar = pltpu.get_barrier_semaphore()
-
-    def greet(dev):
-        pl.semaphore_signal(bar, inc=1, device_id=(g, dev), device_id_type=MESH)
-
-    for s in (h, HEADS + h, 2 * HEADS + 2 * h, 2 * HEADS + 2 * h + 1):
-        pl.when(s != d)(functools.partial(greet, s))
-    for b in peers:
-        greet(HEADS * p + b)
-    pl.when(p > 0)(functools.partial(greet, d - HEADS))
     count = 2 * HEADS - 1 + jnp.where(p < planes - 1, 1, 0) - jnp.where(hd == h, 1, 0)
     pl.semaphore_wait(bar, count)
 
@@ -422,14 +432,17 @@
 def worker_body(qkv, igate, fgate, doc_start, lengths):
     width = igate.shape[1]
     span = HEADS * width
-    vm = pl.BlockSpec(memory_space=pltpu.VMEM)
+    anywhere = pl.BlockSpec(memory_space=pl.ANY)
     dma = pltpu.SemaphoreType.DMA
     return pl.pallas_call(
         worker_kernel,
         out_shape=jax.ShapeDtypeStruct((width, HEADS * DV), bf16),
-        in_specs=[pl.BlockSpec(memory_space=pl.ANY), vm, vm, vm, pl.BlockSpec(memory_space=pltpu.SMEM)],
+        in_specs=[anywhere] * 4 + [pl.BlockSpec(memory_space=pltpu.SMEM)],
         out_specs=pl.BlockSpec(memory_space=pl.ANY),
         scratch_shapes=[
+            pltpu.VMEM((HEADS, width), f32),
+            pltpu.VMEM((HEADS, width), f32),
+            pltpu.VMEM((1, width), jnp.int32),
             pltpu.VMEM((4, DK, span), bf16),
             pltpu.VMEM((HEADS, 8, width), f32),
             pltpu.VMEM((HEADS, 8, width), f32),
@@ -443,10 +456,10 @@
             pltpu.VMEM((24, DK), f32),
             pltpu.VMEM((HEADS, width, DV), bf16),
             dma((HEADS,)), dma((4,)), dma((HEADS - 1,)), dma((HEADS,)),
-            dma((PARTS + 1,)), dma((PARTS + 1,)), dma((HEADS,)), dma((HEADS,)),
+            dma((PARTS + 1,)), dma((PARTS + 1,)), dma((HEADS,)), dma((HEADS,)), dma((3,)),
         ],
         compiler_params=pltpu.CompilerParams(
-            collective_id=0, has_side_effects=True, vmem_limit_bytes=40 * 1024 * 1024
+            collective_id=0, has_side_effects=True, vmem_limit_bytes=60 * 1024 * 1024
         ),
     )(qkv, igate, fgate, doc_start.reshape(1, width), lengths)
 

time: 49.8 us -> 48.8 us (0.980)
  local copies, waits for them, and re-layouts: 3.35 us -> 1.88 us
  Pallas kernels: 45.5 us -> 46.1 us
    unnamed x9 -> x1, local copies, waits for them, and re-layouts: 3.35 us -> 1.88 us
    pallas_call x1, Pallas kernels: 45.5 us -> 46.1 us  [worker_body(): pl.pallas_call(worker_kernel, out_shape=jax.ShapeDtypeStruct((width, HEAD...]
where the time goes in v2:
time: 48.8 us; the launch traced here: 48.6 us
  Pallas kernels  46.1 us (94%)
  local copies, waits for them, and re-layouts  1.88 us (4%)
  between operations  0.66 us (1%)
    pallas_call x1, Pallas kernels, worker_body(): pl.pallas_call(worker_kernel, out_shape=jax.ShapeDtypeStruct((width, HEAD...  46.1 us
    unnamed x1, local copies, waits for them, and re-layouts  1.88 us

profile of v2, /device:TPU:29, one launch (start us, length us, event | category | flops | bytes accessed | tf_op | source)
XLA Modules:
  0.0 48.6 jit_solution(5834611816458277942)
XLA Ops:
  0.7 46.1 %shard_map.55 = bf16[128,2048]{1,0:T(8,128)(2,1)} custom-call(bf16[256,2048]{1,0:T(8,128)(2,1)} %qkv.1, f32[4,128]{1,0:T(4,128)} %ig_hbm.1, f32[4,128]{1,0:T(4,128)} %fg_hbm.1, s32[1,128]{1,0:T(1,128)} %bitcast.1, s32[1]{0:T(128)S(6)} %copy.7.live_len), custom_call_target="tpu_custom_call" | custom-call | tf_op jit(solution)/shard_map/pallas_call | solution.py:437
  46.7 1.9 %copy.8 = bf16[128,2048]{1,0:T(8,128)(2,1)} copy(bf16[128,2048]{1,0:T(8,128)(2,1)} %shard_map.55) | data formatting | bytes 1048576

commit v3 on v2

--- a/solution.py
+++ b/solution.py
@@ -260,7 +260,7 @@
             qkv.at[:, pl.ds(j * span, span)], inbox.at[role], insend.at[j], inrecv.at[role], HEADS * j + hd
         )
 
-    for j in range(planes):
+    def send(j):
         away = HEADS * j + hd != d
 
         @pl.when(away)
@@ -272,6 +272,13 @@
             pltpu.make_async_copy(
                 qkv.at[:, pl.ds(j * span, span)], inbox.at[role], inrecv.at[role]
             ).start()
+
+    def send_rest():
+        for j in range(1, planes):
+            send(j)
+
+    send(0)
+    pl.when(big == 0)(send_rest)
 
     def landed(slot):
         pltpu.make_async_copy(inbox.at[slot], inbox.at[slot], inrecv.at[slot]).wait()
@@ -304,6 +311,7 @@
     u = jnp.where(tail, jnp.exp(cl - mu), 0.0)
     sq_sum = jnp.sum(u * u, axis=1, keepdims=True)
     key_scale = DK ** (-0.5)
+    pl.when(big > 0)(send_rest)
 
     def own():
         landed(0)

time: 48.8 us -> 48.8 us (level)
  no operation moved by 1% of the time
where the time goes in v3:
time: 48.8 us; the launch traced here: 48.6 us
  Pallas kernels  46.1 us (94%)
  local copies, waits for them, and re-layouts  1.88 us (4%)
  between operations  0.66 us (1%)
    pallas_call x1, Pallas kernels, worker_body(): pl.pallas_call(worker_kernel, out_shape=jax.ShapeDtypeStruct((width, HEAD...  46.1 us
    unnamed x1, local copies, waits for them, and re-layouts  1.88 us

profile of v3, /device:TPU:29, one launch (start us, length us, event | category | flops | bytes accessed | tf_op | source)
XLA Modules:
  0.0 48.6 jit_solution(14425841859337468621)
XLA Ops:
  0.7 46.1 %shard_map.55 = bf16[128,2048]{1,0:T(8,128)(2,1)} custom-call(bf16[256,2048]{1,0:T(8,128)(2,1)} %qkv.1, f32[4,128]{1,0:T(4,128)} %ig_hbm.1, f32[4,128]{1,0:T(4,128)} %fg_hbm.1, s32[1,128]{1,0:T(1,128)} %bitcast.1, s32[1]{0:T(128)S(6)} %copy.7.live_len), custom_call_target="tpu_custom_call" | custom-call | tf_op jit(solution)/shard_map/pallas_call | solution.py:445
  46.7 1.9 %copy.8 = bf16[128,2048]{1,0:T(8,128)(2,1)} copy(bf16[128,2048]{1,0:T(8,128)(2,1)} %shard_map.55) | data formatting | bytes 1048576

commit v4 on v2

--- a/solution.py
+++ b/solution.py
@@ -194,7 +194,7 @@
 
 def worker_kernel(
     qkv, ig_hbm, fg_hbm, doc_hbm, live_len, out,
-    ig, fg, doc, inbox, meta, metain, wts, qt, num, den, st_in, st_out, sm_in, sm_out, obuf,
+    ig, fg, doc, inbox, meta, metain, top, sq_own, qt, num, den, st_in, st_out, sm_in, sm_out, obuf,
     insend, inrecv, msend, mrecv, csend, crecv, osend, orecv, lsem,
 ):
     planes = HEADS
@@ -279,23 +279,26 @@
     for i, b in enumerate(peers):
         pltpu.make_async_copy(metain.at[b], metain.at[b], mrecv.at[b]).wait()
 
-    rows = jnp.concatenate([metain[b] for b in range(planes)], axis=1)
-    ig_row, a_row, doc_row, live_row = (rows[i : i + 1, :] for i in range(4))
-    ti = lax.broadcasted_iota(jnp.int32, (span, span), 0)
-    si = lax.broadcasted_iota(jnp.int32, (span, span), 1)
-    tri = ti >= si
+    ti = lax.broadcasted_iota(jnp.int32, (width, width), 0)
+    si = lax.broadcasted_iota(jnp.int32, (width, width), 1)
     eye = ti == si
-    b_col = jnp.sum(jnp.where(tri, a_row, 0.0), axis=1, keepdims=True)
-    r_col = jnp.sum(jnp.where(tri, doc_row, 0.0), axis=1, keepdims=True)
-    live_col = jnp.sum(jnp.where(eye, live_row, 0.0), axis=1, keepdims=True)
-    b_row = jnp.sum(jnp.where(eye, b_col, 0.0), axis=0, keepdims=True)
-    r_row = jnp.sum(jnp.where(eye, r_col, 0.0), axis=0, keepdims=True)
-    allowed = tri & (r_col == r_row) & (live_row > 0.5)
-    ex = jnp.where(allowed, b_col - b_row + ig_row, empty_max)
-    top = jnp.max(ex, axis=1, keepdims=True)
-    weights = jnp.where(allowed, jnp.exp(ex - top), 0.0)
-    wts[...] = weights
-    sq_own = jnp.sum(weights * weights, axis=1, keepdims=True)
+
+    def upright(row):
+        return jnp.sum(jnp.where(eye, row, 0.0), axis=1, keepdims=True)
+
+    b_cols, r_cols, live_cols, b_rows, r_rows = [], [], [], [], []
+    b_last = r_last = jnp.zeros((1, 1), f32)
+    for i in range(planes):
+        gates = metain[i]
+        for at, last, cols, lines in ((1, b_last, b_cols, b_rows), (2, r_last, r_cols, r_rows)):
+            col = last + jnp.sum(jnp.where(ti >= si, gates[at : at + 1], 0.0), axis=1, keepdims=True)
+            cols.append(col)
+            lines.append(jnp.sum(jnp.where(eye, col, 0.0), axis=0, keepdims=True))
+        b_last, r_last = b_rows[-1][:, width - 1 :], r_rows[-1][:, width - 1 :]
+        live_cols.append(upright(gates[3:4]))
+    b_row, r_row = jnp.concatenate(b_rows, axis=1), jnp.concatenate(r_rows, axis=1)
+    ig_row = jnp.concatenate([metain[i, 0:1, :] for i in range(planes)], axis=1)
+    live_row = jnp.concatenate([metain[i, 3:4, :] for i in range(planes)], axis=1)
     b_end = b_row[:, span - 1 : span]
     r_end = r_row[:, span - 1 : span]
     tail = (r_row == r_end) & (live_row > 0.5)
@@ -310,12 +313,21 @@
         qt[...] = inbox[0].astype(f32).T.astype(bf16)
         for b in range(planes):
             r = pl.ds(b * width, width)
-            score = jnp.dot(qt[r, :], inbox[1], preferred_element_type=f32) * key_scale
-            w = wts[r, :] * score
+            wide = (b + 1) * width
+            row_at = b * width + lax.broadcasted_iota(jnp.int32, (width, wide), 0)
+            col_at = lax.broadcasted_iota(jnp.int32, (width, wide), 1)
+            allowed = (row_at >= col_at) & (r_cols[b] == r_row[:, :wide]) & (live_row[:, :wide] > 0.5)
+            ex = jnp.where(allowed, b_cols[b] - b_row[:, :wide] + ig_row[:, :wide], empty_max)
+            highest_ex = jnp.max(ex, axis=1, keepdims=True)
+            weights = jnp.where(allowed, jnp.exp(ex - highest_ex), 0.0)
+            top[r, :] = highest_ex
+            sq_own[r, :] = jnp.sum(weights * weights, axis=1, keepdims=True)
+            score = jnp.dot(qt[r, :], inbox[1, :, 0:wide], preferred_element_type=f32) * key_scale
+            w = weights * score
             den[r, :] = jnp.sum(w, axis=1, keepdims=True)
             wb = w.astype(bf16)
             for f in range(2):
-                num[r, pl.ds(f * DK, DK)] = dot_nt(wb, inbox[2 + f])
+                num[r, pl.ds(f * DK, DK)] = dot_nt(wb, inbox[2 + f, :, 0:wide])
 
     @pl.when(p == 0)
     def _():
@@ -382,17 +394,17 @@
         )
 
     for b in range(planes):
-        lo, r = b * width, pl.ds(b * width, width)
-        first = r_col[lo : lo + width] < 0.5
-        f = jnp.where(first, b_col[lo : lo + width] + m_in, empty_max)
-        mx = top[lo : lo + width]
+        r = pl.ds(b * width, width)
+        first = r_cols[b] < 0.5
+        f = jnp.where(first, b_cols[b] + m_in, empty_max)
+        mx = top[r, :]
         m = jnp.maximum(mx, f)
         xs = jnp.exp(mx - m)
         ys = jnp.where(first, jnp.exp(f - m), 0.0)
         qb = qt[r, :]
         dn = xs * den[r, :] + ys * dot_nt(qb, nb)[:, 0:1]
-        sq = xs * xs * sq_own[lo : lo + width] + ys * ys * sq_in
-        lv = live_col[lo : lo + width] > 0.5
+        sq = xs * xs * sq_own[r, :] + ys * ys * sq_in
+        lv = live_cols[b] > 0.5
         inv = 1.0 / jnp.where(lv, jnp.maximum(jnp.abs(dn), jnp.sqrt(sq)), 1.0)
         for c in range(PARTS):
             cs = pl.ds(c * 128, 128)
@@ -446,7 +458,8 @@
             pltpu.VMEM((4, DK, span), bf16),
             pltpu.VMEM((HEADS, 8, width), f32),
             pltpu.VMEM((HEADS, 8, width), f32),
-            pltpu.VMEM((span, span), f32),
+            pltpu.VMEM((span, 1), f32),
+            pltpu.VMEM((span, 1), f32),
             pltpu.VMEM((span, DK), bf16),
             pltpu.VMEM((span, DV), f32),
             pltpu.VMEM((span, 1), f32),

time: 48.8 us -> 48.9 us (level)
  no operation moved by 1% of the time
where the time goes in v4:
time: 48.9 us; the launch traced here: 48.8 us
  Pallas kernels  46.2 us (94%)
  local copies, waits for them, and re-layouts  1.88 us (4%)
  between operations  0.66 us (1%)
    pallas_call x1, Pallas kernels, worker_body(): pl.pallas_call(worker_kernel, out_shape=jax.ShapeDtypeStruct((width, HEAD...  46.2 us
    unnamed x1, local copies, waits for them, and re-layouts  1.88 us

profile of v4, /device:TPU:29, one launch (start us, length us, event | category | flops | bytes accessed | tf_op | source)
XLA Modules:
  0.0 48.8 jit_solution(13949626543277633344)
XLA Ops:
  0.7 46.2 %shard_map.55 = bf16[128,2048]{1,0:T(8,128)(2,1)} custom-call(bf16[256,2048]{1,0:T(8,128)(2,1)} %qkv.1, f32[4,128]{1,0:T(4,128)} %ig_hbm.1, f32[4,128]{1,0:T(4,128)} %fg_hbm.1, s32[1,128]{1,0:T(1,128)} %bitcast.1, s32[1]{0:T(128)S(6)} %copy.7.live_len), custom_call_target="tpu_custom_call" | custom-call | tf_op jit(solution)/shard_map/pallas_call | solution.py:449
  46.9 1.9 %copy.8 = bf16[128,2048]{1,0:T(8,128)(2,1)} copy(bf16[128,2048]{1,0:T(8,128)(2,1)} %shard_map.55) | data formatting | bytes 1048576

commit v5 on v4

--- a/solution.py
+++ b/solution.py
@@ -260,7 +260,7 @@
             qkv.at[:, pl.ds(j * span, span)], inbox.at[role], insend.at[j], inrecv.at[role], HEADS * j + hd
         )
 
-    for j in range(planes):
+    def send(j):
         away = HEADS * j + hd != d
 
         @pl.when(away)
@@ -272,6 +272,13 @@
             pltpu.make_async_copy(
                 qkv.at[:, pl.ds(j * span, span)], inbox.at[role], inrecv.at[role]
             ).start()
+
+    def send_rest():
+        for j in range(1, planes):
+            send(j)
+
+    send(0)
+    pl.when(big == 0)(send_rest)
 
     def landed(slot):
         pltpu.make_async_copy(inbox.at[slot], inbox.at[slot], inrecv.at[slot]).wait()
@@ -308,6 +315,11 @@
     sq_sum = jnp.sum(u * u, axis=1, keepdims=True)
     key_scale = DK ** (-0.5)
 
+    @pl.when(big > 0)
+    def _():
+        feature(0).wait_send()
+        send_rest()
+
     def own():
         landed(0)
         qt[...] = inbox[0].astype(f32).T.astype(bf16)
@@ -426,7 +438,7 @@
         c.wait_send()
     for j in range(planes):
 
-        @pl.when(HEADS * j + hd != d)
+        @pl.when((HEADS * j + hd != d) & (big * (planes - j) < planes))
         def _():
             feature(j).wait_send()
 

time: 48.9 us -> 49.2 us (level)
  no operation moved by 1% of the time
where the time goes in v5:
time: 49.2 us; the launch traced here: 48.6 us
  Pallas kernels  46.1 us (94%)
  local copies, waits for them, and re-layouts  1.88 us (4%)
  between operations  0.66 us (1%)
    pallas_call x1, Pallas kernels, worker_body(): pl.pallas_call(worker_kernel, out_shape=jax.ShapeDtypeStruct((width, HEAD...  46.1 us
    unnamed x1, local copies, waits for them, and re-layouts  1.88 us

profile of v5, /device:TPU:29, one launch (start us, length us, event | category | flops | bytes accessed | tf_op | source)
XLA Modules:
  0.0 48.6 jit_solution(6287291761224393207)
XLA Ops:
  0.7 46.1 %shard_map.55 = bf16[128,2048]{1,0:T(8,128)(2,1)} custom-call(bf16[256,2048]{1,0:T(8,128)(2,1)} %qkv.1, f32[4,128]{1,0:T(4,128)} %ig_hbm.1, f32[4,128]{1,0:T(4,128)} %fg_hbm.1, s32[1,128]{1,0:T(1,128)} %bitcast.1, s32[1]{0:T(128)S(6)} %copy.7.live_len), custom_call_target="tpu_custom_call" | custom-call | tf_op jit(solution)/shard_map/pallas_call | solution.py:461
  46.7 1.9 %copy.8 = bf16[128,2048]{1,0:T(8,128)(2,1)} copy(bf16[128,2048]{1,0:T(8,128)(2,1)} %shard_map.55) | data formatting | bytes 1048576

commit v6 on v2

--- a/solution.py
+++ b/solution.py
@@ -194,7 +194,7 @@
 
 def worker_kernel(
     qkv, ig_hbm, fg_hbm, doc_hbm, live_len, out,
-    ig, fg, doc, inbox, meta, metain, wts, qt, num, den, st_in, st_out, sm_in, sm_out, obuf,
+    ig, fg, doc, inbox, meta, metain, wts, qt, num, den, state, st_in, st_out, sm_in, sm_out, obuf,
     insend, inrecv, msend, mrecv, csend, crecv, osend, orecv, lsem,
 ):
     planes = HEADS
@@ -329,6 +329,15 @@
     n8 = dot_nt(jnp.ones((8, span), bf16), keyw)
     landed(2)
     landed(3)
+
+    def product(c):
+        return dot_nt(keyw, inbox[2 + c // 2, pl.ds((c % 2) * 128, 128), :])
+
+    @pl.when((p > 0) & (p < planes - 1))
+    def _():
+        for c in range(PARTS):
+            state[c] = product(c)
+
     pl.when(p >= 2)(own)
 
     sm_copy = remote(sm_out, sm_in, csend.at[PARTS], crecv.at[PARTS], d + HEADS)
@@ -360,10 +369,14 @@
         def _():
             pltpu.make_async_copy(st_in.at[c], st_in.at[c], crecv.at[c]).wait()
 
-        @pl.when(p < planes - 1)
-        def _():
-            vals = inbox[2 + c // 2, pl.ds((c % 2) * 128, 128), :]
-            st_out[c] = (late * dot_nt(keyw, vals) + early * st_in[c].astype(f32)).astype(bf16)
+        @pl.when(p == 0)
+        def _():
+            st_out[c] = (late * product(c)).astype(bf16)
+            st_copies[c].start()
+
+        @pl.when((p > 0) & (p < planes - 1))
+        def _():
+            st_out[c] = (late * state[c] + early * st_in[c].astype(f32)).astype(bf16)
             st_copies[c].start()
 
     pl.when(p < 2)(own)
@@ -450,6 +463,7 @@
             pltpu.VMEM((span, DK), bf16),
             pltpu.VMEM((span, DV), f32),
             pltpu.VMEM((span, 1), f32),
+            pltpu.VMEM((PARTS, DK, 128), f32),
             pltpu.VMEM((PARTS, DK, 128), bf16),
             pltpu.VMEM((PARTS, DK, 128), bf16),
             pltpu.VMEM((24, DK), f32),

time: 48.8 us -> 49.1 us (level)
  no operation moved by 1% of the time
where the time goes in v6:
time: 49.1 us; the launch traced here: 48.9 us
  Pallas kernels  46.4 us (95%)
  local copies, waits for them, and re-layouts  1.88 us (4%)
  between operations  0.66 us (1%)
    pallas_call x1, Pallas kernels, worker_body(): pl.pallas_call(worker_kernel, out_shape=jax.ShapeDtypeStruct((width, HEAD...  46.4 us
    unnamed x1, local copies, waits for them, and re-layouts  1.88 us

profile of v6, /device:TPU:29, one launch (start us, length us, event | category | flops | bytes accessed | tf_op | source)
XLA Modules:
  0.0 48.9 jit_solution(171862601669415603)
XLA Ops:
  0.7 46.4 %shard_map.55 = bf16[128,2048]{1,0:T(8,128)(2,1)} custom-call(bf16[256,2048]{1,0:T(8,128)(2,1)} %qkv.1, f32[4,128]{1,0:T(4,128)} %ig_hbm.1, f32[4,128]{1,0:T(4,128)} %fg_hbm.1, s32[1,128]{1,0:T(1,128)} %bitcast.1, s32[1]{0:T(128)S(6)} %copy.7.live_len), custom_call_target="tpu_custom_call" | custom-call | tf_op jit(solution)/shard_map/pallas_call | solution.py:450
  47.0 1.9 %copy.8 = bf16[128,2048]{1,0:T(8,128)(2,1)} copy(bf16[128,2048]{1,0:T(8,128)(2,1)} %shard_map.55) | data formatting | bytes 1048576
